TPU v7x, 256 devices: a whole 4x4x8 slice. The times are simulated.
256 devices in a mesh: dp: 2 (over y_hi), expert: 128 (over y_lo, z, x, core).
Axes of the slice: x: 4, y: 4 (y_hi: 2, y_lo: 2; y = y_hi * 2 + y_lo), z: 8, core: 2. Of those that a mesh axis runs over, the one named last changes fastest.
Arguments:
- patches: bfloat16 [65536, 768], P(('dp', 'expert')), may hold values from -8 to 8
- slot_keys: bfloat16 [512, 768], P('expert'), may hold values from -2 to 2
- expert_in: bfloat16 [128, 768, 2560], P('expert', None, 'dp'), may hold values from -0.21875 to 0.21875
- expert_out: bfloat16 [128, 2560, 768], P('expert', 'dp'), may hold values from -0.125 to 0.125
- out_grad: bfloat16 [65536, 768], P(('dp', 'expert')), may hold values from -6 to 6
Outputs:
- layer_out: bfloat16 [65536, 768], P(('dp', 'expert'))
- patch_grad: bfloat16 [65536, 768], P(('dp', 'expert'))
- slot_key_grad: float32 [512, 768], P('expert')
- expert_in_grad: bfloat16 [128, 768, 2560], P('expert', None, 'dp')
- expert_out_grad: bfloat16 [128, 2560, 768], P('expert', 'dp')
All inputs are finite; a program needn't handle non-finite values.
Results may differ from a plain program's by a relative error of at most 0.02.
Values may be sent and summed in bfloat16 or wider, within the bound.
No kernel may reach another device: no remote copies, remote signals or barrier semaphores. Data moves between devices by JAX's collectives and lax.ppermute only.
A program may use at most 128 MiB of HBM per device.

v0:
```python
import jax
import jax.numpy as jnp
from jax import lax
from jax.experimental import pallas as pl
from jax.experimental.pallas import tpu as pltpu
from jax.sharding import Mesh, PartitionSpec as P

D = 768
SLOTS = 4
BF = jnp.bfloat16
F32 = jnp.float32
EXPERT = ("yl", "z", "x", "core")
TOKEN = ("dp",) + EXPERT
ROUTE = ("core", "z", "x")
PLANE = ("z", "x", "yl")
TILE = 256
WIDE, TIGHT = 46 * 1024 * 1024, 52 * 1024 * 1024
SPARE = 8000000
MICRO = 1000000000
CUBIC = 0.044715
ROOT = 0.7978845608028654


def mm(left, right, contract):
    return lax.dot_general(left, right, (contract, ((), ())), preferred_element_type=F32)


def dot(left, right):
    return mm(left, right, ((1,), (0,)))


def dot_rows(left, right):
    return mm(left, right, ((0,), (0,)))


def dot_last(left, right):
    return mm(left, right, ((1,), (1,)))


class Far:
    def __init__(self, there, here, sems, first_sem, cuts, by_rows, start):
        self.there, self.here, self.sems, self.first_sem = there, here, sems, first_sem
        self.cuts, self.by_rows, self.start = cuts, by_rows, start

    def copy(self, piece, out):
        rows, cols = self.here.shape
        start, stop = self.cuts[piece] if self.cuts else (0, cols)
        at = (pl.ds(0, rows), pl.ds(start, stop - start))
        if self.by_rows:
            at = (pl.ds(start, stop - start), pl.ds(0, cols))
        near = self.here.at[at]
        far = self.there.at[at[0], pl.ds(self.start + start, stop - start)] if self.start else self.there.at[at]
        source, target = (near, far) if out else (far, near)
        return pltpu.make_async_copy(source, target, self.sems.at[self.first_sem + piece])

    def fetch(self, *pieces):
        for piece in pieces or (0,):
            self.copy(piece, False).start()

    def get(self, piece=0):
        self.copy(piece, False).wait()
        start, stop = self.cuts[piece] if self.cuts else (0, self.here.shape[1])
        return self.here[:, start:stop]

    def put(self, value, piece=0):
        start, stop = self.cuts[piece] if self.cuts else (0, self.here.shape[1])
        self.here[:, start:stop] = value
        self.copy(piece, True).start()

    def wait(self):
        for piece in range(len(self.cuts or (0,))):
            self.copy(piece, True).wait()


HERE = pl.BlockSpec(memory_space=pltpu.VMEM)
FLAG = pl.BlockSpec(memory_space=pltpu.SMEM)
THERE = pl.BlockSpec(memory_space=pl.ANY)


class In:
    def __init__(self, value, rows=None, cuts=None, by_rows=False, start=0, width=None):
        self.value, self.cuts, self.by_rows, self.start = value, cuts, by_rows, start
        self.shape = (rows or value.shape[0], width or value.shape[1])


class After:
    def __init__(self, value):
        self.value = value


class Out:
    def __init__(self, shape, dtype, cuts=None, room=False, by_rows=False):
        self.shape, self.dtype, self.cuts, self.by_rows = shape, dtype, cuts, by_rows
        width = shape[1] * jnp.dtype(dtype).itemsize
        self.rows = max(shape[0], -(-SPARE // width) // 256 * 256 + 256) if room else shape[0]


def call(kernel, name, cost, outs, *operands, limit=WIDE):
    values, specs, scratch, plan, sems = [], [], [], [], 0

    def far(shape, dtype, cuts, by_rows, start=0):
        nonlocal sems
        scratch.append(pltpu.VMEM(shape, dtype))
        sems += len(cuts or (0,))
        return len(scratch) - 1, sems - len(cuts or (0,)), cuts, by_rows, start

    for operand in operands:
        if isinstance(operand, In):
            values.append(operand.value)
            specs.append(THERE)
            plan.append(far(operand.shape, operand.value.dtype, operand.cuts, operand.by_rows, operand.start))
        elif isinstance(operand, After):
            values.append(operand.value)
            specs.append(THERE)
            plan.append(None)
        else:
            value, spec = operand if isinstance(operand, tuple) else (operand, HERE)
            values.append(value)
            specs.append(spec)
            plan.append(())
    shapes, out_specs = [], []
    for out in outs:
        if isinstance(out, Out):
            shapes.append(jax.ShapeDtypeStruct((out.rows, out.shape[1]), out.dtype))
            out_specs.append(THERE)
            plan.append(far(out.shape, out.dtype, out.cuts, out.by_rows))
        else:
            shapes.append(jax.ShapeDtypeStruct(*out))
            out_specs.append(HERE)
            plan.append(())

    def run(*refs):
        inner, waiting = [], []
        mine = refs[len(values) + len(outs) :]
        for at, (ref, how) in enumerate(zip(refs, plan)):
            if how is None:
                continue
            if how == ():
                inner.append(ref)
                continue
            inner.append(Far(ref, mine[how[0]], mine[-1], *how[1:]))
            if at >= len(values):
                waiting.append(inner[-1])
        kernel(*inner)
        for one in waiting:
            one.wait()

    return pl.pallas_call(
        run,
        name=name,
        out_shape=shapes,
        in_specs=specs,
        out_specs=out_specs,
        scratch_shapes=scratch + ([pltpu.SemaphoreType.DMA((sems,))] if sems else []),
        compiler_params=pltpu.CompilerParams(vmem_limit_bytes=limit),
        cost_estimate=pl.CostEstimate(flops=cost * MICRO, bytes_accessed=1000, transcendentals=0),
    )(*values)


def flat(ref):
    value = ref[...].astype(F32)
    return value.reshape(value.shape[0] * value.shape[1], D).astype(BF)


def split(value, yl):
    low, high = value[:, :SLOTS, :], value[:, SLOTS:, :]
    rows = value.shape[0] * SLOTS
    ours = jnp.where(yl == 0, low, high).reshape(rows, D)
    theirs = jnp.where(yl == 0, high, low).reshape(rows, D)
    return ours, theirs


def merge(ours, theirs, yl):
    groups = (ours.shape[0] // SLOTS, SLOTS, D)
    ours, theirs = ours.reshape(groups), theirs.reshape(groups)
    low, high = jnp.where(yl == 0, ours, theirs), jnp.where(yl == 0, theirs, ours)
    return jnp.concatenate([low, high], axis=1)


def softmax(scores, axis):
    raised = jnp.exp(scores - jnp.max(scores, axis=axis, keepdims=True))
    return raised / jnp.sum(raised, axis=axis, keepdims=True)


def softmax_back(share, share_grad, axis):
    return share * (share_grad - jnp.sum(share_grad * share, axis=axis, keepdims=True))


def front(place, patches, own, other, rows, dispatch, keys):
    patches.fetch()
    core = place[0]
    for at, block in ((core, own), (1 - core, other)):
        keys.here[pl.ds(pl.multiple_of(at * 256, 256), 256), :] = flat(block)
    keys.copy(0, True).start()
    image = patches.get()
    share = softmax(dot_last(image, keys.here[...]), 0)
    dispatch.put(share)
    rows.put(dot_rows(share.astype(BF), image).astype(BF))


def front_grads(patches, keys, out_grad, grads, combine):
    patches.fetch()
    keys.fetch()
    out_grad.fetch()
    share = softmax(dot_last(patches.get(), keys.get()), 1)
    combine.put(share)
    grads.put(dot_rows(share.astype(BF), out_grad.get()).astype(BF))


def part_ways(place, routed, ours, theirs):
    near, far = split(routed[...].astype(F32), place[1])
    ours[...] = near.astype(BF)
    theirs[...] = far.astype(BF)


def begin(*fars):
    for piece in range(2):
        for far in fars:
            far.fetch(piece)


def arrived(step, *fars):
    if step < 2:
        for far in fars:
            far.copy(step, False).wait()


def load(first, second, first_here, second_here, sems):
    copies = [
        pltpu.make_async_copy(first, first_here, sems.at[0]),
        pltpu.make_async_copy(second, second_here, sems.at[1]),
    ]
    for copy in copies:
        copy.start()
    for copy in copies:
        copy.wait()


def forward(*refs):
    blocks = (len(refs) - 3) // 2
    low, first, second, outs, acts = refs[:blocks], *refs[blocks : blocks + 2], refs[-blocks - 1 : -1], refs[-1]
    here = jnp.concatenate([ref[...] for ref in low], axis=0)
    acts.put(here, 0)
    total = None
    for step in range(first.shape[1] // TILE):
        part = slice(step * TILE, step * TILE + TILE)
        value = dot(here, first[:, part])
        square = value * value
        bend = jnp.tanh(ROOT * value * (1.0 + CUBIC * square))
        gate = 0.5 + 0.5 * bend
        active = (value * gate).astype(BF)
        acts.put(active, 1 + step)
        rise = (0.5 * ROOT) * value * (1.0 - bend * bend) * (1.0 + (3.0 * CUBIC) * square)
        acts.put((gate + rise).astype(BF), 1 + first.shape[1] // TILE + step)
        term = dot(active, second[part, :])
        total = term if total is None else total + term
    for at, out in enumerate(outs):
        out[...] = total[at * 256 : at * 256 + 256].astype(out.dtype)


def backward(*refs):
    blocks = (len(refs) - 4) // 2
    low, first, second, slope, outs, kept = (
        refs[:blocks], *refs[blocks : blocks + 3], refs[-blocks - 1 : -1], refs[-1],
    )
    far = [one for one in (second, slope, first) if isinstance(one, Far)]
    begin(*far)
    first, second = (one.here if isinstance(one, Far) else one for one in (first, second))
    here = jnp.concatenate([ref[...] for ref in low], axis=0)
    kept.put(here, 0)
    total = None
    for step in range(first.shape[1] // TILE):
        arrived(step, *far)
        part = slice(step * TILE, step * TILE + TILE)
        rounded = (dot_last(here, second[part, :]) * slope.here[:, part].astype(F32)).astype(BF)
        kept.put(rounded, 1 + step)
        term = dot_last(rounded, first[:, part])
        total = term if total is None else total + term
    for at, out in enumerate(outs):
        out[...] = total[at * 256 : at * 256 + 256].astype(out.dtype)


def weight_grad(steps, into, *refs):
    acts, kept, out, done = refs[:3], refs[3:6], refs[6], refs[7]
    done[...] = jnp.zeros((8, 128), F32)
    narrow = [1 + step for step in range(steps)] if not into else [0]
    other = [0] if not into else [1 + step for step in range(steps)]
    for step in range(steps):
        for act, keep in zip(acts, kept):
            if step == 0 or not into:
                act.fetch(narrow[0 if into else step])
            if step == 0 or into:
                keep.fetch(other[step if into else 0])
    held = [(keep if not into else act).get(0) for act, keep in zip(acts, kept)]
    for step in range(steps):
        part = slice(step * TILE, step * TILE + TILE)
        total = None
        for act, keep, one in zip(acts, kept, held):
            moving = keep.get(other[step]) if into else act.get(narrow[step])
            term = dot_rows(one, moving) if into else dot_rows(moving, one)
            total = term if total is None else total + term
        if into:
            out[:, part] = total.astype(BF)
        else:
            out[part, :] = total.astype(BF)


def join(place, ours, ours_far, theirs, theirs_far, out):
    near = ours[...] + ours_far[...].astype(F32)
    far = theirs[...].astype(F32) + theirs_far[...].astype(F32)
    out[...] = merge(near, far, place[1]).astype(BF)


def middle(slot_output, out_grad, combine, layer_out, mix):
    out_grad.fetch()
    combine.fetch()
    grad = dot_last(out_grad.get(), slot_output[...])
    share = combine.get()
    mix.put(softmax_back(share, grad, 1))
    layer_out.put(dot(share.astype(BF), slot_output[...]).astype(BF))


def last(place, slot_in_grad, patches, dispatch, mix, score_grad, kept, sent, term):
    patches.fetch()
    dispatch.fetch()
    mix.fetch()
    image = patches.get()
    grad = dot_last(image, slot_in_grad[...])
    change = softmax_back(dispatch.get(), grad, 0)
    score = (mix.get() + change).astype(BF)
    score_grad.put(score)
    term[...] = dot_rows(score, image)
    core = place[0]
    kept[...] = term[pl.ds(pl.multiple_of(core * 256, 256), 256), :]
    sent[...] = term[pl.ds(pl.multiple_of((1 - core) * 256, 256), 256), :].astype(BF)


def fold(mine, other, out):
    out[...] = (mine[...] + other[...].astype(F32)).reshape(64, SLOTS, D).astype(BF)


def patch_back(dispatch, slots, score_grad, keys, out):
    dispatch.fetch()
    score_grad.fetch()
    keys.fetch()
    total = dot(dispatch.get().astype(BF), slots[...])
    out.put((total + dot(score_grad.get(), keys.get())).astype(BF))


def swap(value, axis):
    return lax.ppermute(value, axis, [(0, 1), (1, 0)])


def hop(value, flips):
    return lax.ppermute(value, ("dp", "yl"), [(at, at ^ flips) for at in range(4)])


NEXT, ACROSS, AROUND = 1, 2, 3


def exchange(value, axes):
    return lax.all_to_all(value, axes, split_axis=0, concat_axis=0, tiled=True)


def route(rows):
    return exchange(rows.reshape(64, 2 * SLOTS, D), ROUTE)


def local(patches, slot_keys, expert_in, expert_out, out_grad):
    first, second = expert_in[0], expert_out[0]
    half = first.shape[1]
    steps = half // TILE
    place = jnp.stack([lax.axis_index("core"), lax.axis_index("yl")]).astype(jnp.int32)
    place = (place, FLAG)
    block, full, final = ((256, D), BF), ((512, D), BF), ((256, D), F32)
    share = Out((256, 512), F32, room=True)

    own = exchange(jnp.broadcast_to(slot_keys[None], (64, SLOTS, D)), PLANE)
    rows, dispatch, keys = call(
        front, "front", 3, [Out(*full), share, Out(*full, room=True)],
        place, In(patches), own, swap(own, "core"),
    )
    rows = route(rows)
    grads, combine = call(
        front_grads, "front_grads", 2, [Out(*full), share], In(patches), In(keys, 512), In(out_grad)
    )
    early, grads = grads, route(grads)

    def inward(routed, *after):
        return call(part_ways, "part_ways", 1, [block, block], place, routed, *after)

    def weights(after):
        return pl.pallas_call(
            lambda first, second, after, *refs: load(first, second, *refs),
            name="load",
            out_shape=[jax.ShapeDtypeStruct(value.shape, BF) for value in (first, second)],
            in_specs=[THERE] * 3,
            out_specs=[HERE] * 2,
            scratch_shapes=[pltpu.SemaphoreType.DMA((2,))],
            compiler_params=pltpu.CompilerParams(vmem_limit_bytes=WIDE),
            cost_estimate=pl.CostEstimate(flops=1000, bytes_accessed=1000, transcendentals=0),
        )(first, second, after)

    act_cuts, kept_cuts = [(0, D)], [(0, D)]
    for step in range(2 * steps):
        act_cuts += [(D + TILE * step, D + TILE * (step + 1))]
    kept_cuts += act_cuts[1 : 1 + steps]
    slope_at = D + half
    pieces = [(0, TILE), (TILE, half)]
    fetched = In(first, cuts=pieces), In(second, cuts=pieces, by_rows=True)

    def ahead(name, blocks, outs, *after):
        rows = 256 * len(blocks)
        acts = Out((rows, D + 2 * half), BF, act_cuts, room=True)
        return call(forward, name, 60 if name == "forward_across" else 0, outs + [acts], *blocks, *here, *after, limit=WIDE)

    def back(name, blocks, outs, weights, acts, *after):
        rows = 256 * len(blocks)
        kept = Out((rows, D + half), BF, kept_cuts, room=True)
        slope = In(acts, rows, pieces, start=slope_at, width=half)
        cost, limit = (10, WIDE) if weights is here else (30, TIGHT)
        return call(backward, name, cost, outs + [kept], *blocks, *weights, slope, *after, limit=limit)

    def join_up(name, ours, across, near, around, *after):
        (out,) = call(
            join, name, 20, [((64, 2 * SLOTS, D), BF)],
            place, ours, hop(across, ACROSS), hop(near, NEXT), hop(around, AROUND), *after,
        )
        return out

    ours, theirs = inward(rows, After(early))
    here = weights(theirs)
    near_out, around_out, acts_near = ahead(
        "forward_near", [hop(theirs, NEXT), hop(theirs, AROUND)], [block, block]
    )
    across_out, acts_across = ahead(
        "forward_across", [hop(ours, ACROSS)], [block], After(acts_near)
    )
    ours_out, acts_ours = ahead("forward_ours", [ours], [final], After(acts_across))

    ours, theirs = inward(grads, After(acts_ours))
    near, around, across = hop(theirs, NEXT), hop(theirs, AROUND), hop(ours, ACROSS)
    ours_in, kept_ours = back("backward_ours", [ours], [final], here, acts_ours)
    out = join_up("join_out", ours_out, across_out, near_out, around_out, After(kept_ours))
    slot_output = route(out).reshape(512, D)
    near_in, around_in, kept_near = back(
        "backward_near", [near, around], [block, block], fetched, acts_near, After(out)
    )
    across_in, kept_across = back(
        "backward_across", [across], [block], fetched, acts_across, After(kept_near)
    )
    into = join_up("join_in", ours_in, across_in, near_in, around_in, After(slot_output))
    slot_in_grad = route(into).reshape(512, D)

    def weight_sum(name, towards, shape):
        pairs = ((acts_ours, kept_ours, 256), (acts_near, kept_near, 512), (acts_across, kept_across, 256))
        return call(
            lambda *refs: weight_grad(steps, towards, *refs), name, 4, [(shape, BF), ((8, 128), F32)],
            *[In(acts, rows, act_cuts) for acts, _, rows in pairs],
            *[In(kept, rows, kept_cuts) for _, kept, rows in pairs],
        )

    second_grad, second_done = weight_sum("second_grad", False, (half, D))
    first_grad, first_done = weight_sum("first_grad", True, (D, half))

    layer_out, mix = call(
        middle, "middle", 2, [Out(*block), share], slot_output, In(out_grad), In(combine, 256)
    )
    score_grad, kept, sent, _ = call(
        last, "last", 3, [Out((256, 512), BF, room=True), final, block, ((512, D), F32)],
        place, slot_in_grad, In(patches), In(dispatch, 256), In(mix, 256),
        After(first_done), After(second_done),
    )
    (folded,) = call(fold, "fold", 1, [((64, SLOTS, D), BF)], kept, swap(sent, "core"))
    own_total = jnp.sum(exchange(folded, PLANE).astype(F32), axis=0)
    (patch_grad,) = call(
        patch_back, "patch_back", 2, [Out(*block)],
        In(dispatch, 256), slot_in_grad, In(score_grad, 256), In(keys, 512),
    )
    own_total, patch_grad = lax.optimization_barrier((own_total, patch_grad))
    slot_key_grad = own_total + swap(own_total, "dp")
    return layer_out, patch_grad, slot_key_grad, first_grad[None], second_grad[None]


def solution(mesh):
    fine = Mesh(mesh.devices.reshape(2, 2, 8, 4, 2), TOKEN)
    return jax.shard_map(
        local,
        mesh=fine,
        in_specs=(
            P(TOKEN, None),
            P(EXPERT, None),
            P(EXPERT, None, "dp"),
            P(EXPERT, "dp", None),
            P(TOKEN, None),
        ),
        out_specs=(
            P(TOKEN, None),
            P(TOKEN, None),
            P(EXPERT, None),
            P(EXPERT, None, "dp"),
            P(EXPERT, "dp", None),
        ),
        check_vma=False,
    )
```

profile of v0, /device:TPU:24, one launch (start us, length us, event | category | flops | bytes accessed | tf_op | source)
XLA Modules:
  0.0 235.2 jit_solution(9225872182970715090)
XLA Ops:
  1.5 27.5 %all_to_all.30.refs_2_ = bf16[64,4,768]{2,1,0:T(4,128)(2,1)S(1)} all-to-all(bf16[64,4,768]{2,1,0:T(4,128)(2,1)S(1)} %broadcast_in_dim.12), channel_id=1, replica_groups=mesh['dp'=2,'yl'=2,'z'=8,'x'=4,'core'=2] {'z','x','yl'}, dimensions={0} | all-to-all | bytes 786432 | tf_op jit(solution)/shard_map/all_to_all | solution.py:362
  34.5 5.0 %all-to-all-start.1 = ((bf16[64,8,768]{2,1,0:T(8,128)(2,1)}), bf16[64,8,768]{2,1,0:T(8,128)(2,1)S(1)}, u32[]{:S(2)}, u32[]{:S(2)}) async-start(bf16[64,8,768]{2,1,0:T(8,128)(2,1)} %bitcast.2), calls=%async_computation.1 | async-start | bytes 1572864 | tf_op jit(solution)/shard_map/all_to_all | solution.py:362
  39.5 3.3 %front_grads.1 = (bf16[512,768]{1,0:T(8,128)(2,1)}, f32[4096,512]{1,0:T(8,128)}) custom-call(bf16[256,768]{1,0:T(8,128)(2,1)S(1)} %copy-done.7, bf16[5376,768]{1,0:T(8,128)(2,1)} %get-tuple-element.42.refs_1_.refs_3_, bf16[256,768]{1,0:T(8,128)(2,1)S(1)} %copy-done.4), custom_call_target="tpu_custom_call" | custom-call | flops 2000000000 | bytes 1000 | tf_op jit(solution)/shard_map/front_grads/pallas_call | solution.py:148
  42.8 18.6 %all-to-all-done.1.refs_1_ = bf16[64,8,768]{2,1,0:T(8,128)(2,1)S(1)} async-done(((bf16[64,8,768]{2,1,0:T(8,128)(2,1)}), bf16[64,8,768]{2,1,0:T(8,128)(2,1)S(1)}, u32[]{:S(2)}, u32[]{:S(2)}) %all-to-all-start.1) | async-done | bytes 786464 | tf_op jit(solution)/shard_map/all_to_all | solution.py:362
  64.4 3.2 %collective-permute-start.1 = (bf16[256,768]{1,0:T(8,128)(2,1)S(1)}, bf16[256,768]{1,0:T(8,128)(2,1)}, u32[]{:S(2)}, u32[]{:S(2)}) collective-permute-start(bf16[256,768]{1,0:T(8,128)(2,1)S(1)} %get-tuple-element.44.refs_0_), channel_id=1, source_target_pairs={{0,128},{64,192},{128,0},{192,64},{1,129},{65,193},{129,1},{193,65... | collective-permute-start | bytes 1179656 | tf_op jit(solution)/shard_map/ppermute | solution.py:355
  67.6 6.9 %all-to-all-start.2 = ((bf16[64,8,768]{2,1,0:T(8,128)(2,1)}), bf16[64,8,768]{2,1,0:T(8,128)(2,1)S(1)}, u32[]{:S(2)}, u32[]{:S(2)}) async-start(bf16[64,8,768]{2,1,0:T(8,128)(2,1)} %bitcast.5), calls=%async_computation.2 | async-start | bytes 1572864 | tf_op jit(solution)/shard_map/all_to_all | solution.py:362
  78.2 6.7 %forward_near.1 = (bf16[256,768]{1,0:T(8,128)(2,1)}, bf16[256,768]{1,0:T(8,128)(2,1)}, bf16[1280,3328]{1,0:T(8,128)(2,1)}) custom-call(bf16[256,768]{1,0:T(8,128)(2,1)} %collective-permute-done.2.refs_0_, bf16[256,768]{1,0:T(8,128)(2,1)S(1)} %collective-permute-done.3.refs_1_, bf16[768,1280]{1,0:T(8,128)(2,1)S(1)} %get-tuple-element.46.refs_2_.refs_1_, ...), custom_call_target="tpu_custom_call" | custom-call | bytes 1000 | tf_op jit(solution)/shard_map/forward_near/pallas_call | solution.py:148
  86.6 4.6 %forward_across.1 = (bf16[256,768]{1,0:T(8,128)(2,1)}, bf16[1280,3328]{1,0:T(8,128)(2,1)}) custom-call(bf16[256,768]{1,0:T(8,128)(2,1)} %collective-permute-done.1.refs_0_, bf16[768,1280]{1,0:T(8,128)(2,1)S(1)} %get-tuple-element.46.refs_2_.refs_1_, bf16[1280,768]{1,0:T(8,128)(2,1)S(1)} %get-tuple-element.47.refs_3_.refs_2_, ...), custom_call_target="tpu_custom_call" | custom-call | flops 60000002048 | bytes 1000 | tf_op jit(solution)/shard_map/forward_across/pallas_call | solution.py:148
  91.2 2.8 %collective-permute-start.4 = (bf16[256,768]{1,0:T(8,128)(2,1)}, bf16[256,768]{1,0:T(8,128)(2,1)}, u32[]{:S(2)}, u32[]{:S(2)}) collective-permute-start(bf16[256,768]{1,0:T(8,128)(2,1)} %get-tuple-element.51), channel_id=1, source_target_pairs={{0,128},{64,192},{128,0},{192,64},{1,129},{65,193},{129,1},{193,65... | collective-permute-start | bytes 1179656 | tf_op jit(solution)/shard_map/ppermute | solution.py:355
  100.0 3.6 %backward_ours.1 = (f32[256,768]{1,0:T(8,128)S(1)}, bf16[2048,2048]{1,0:T(8,128)(2,1)}) custom-call(bf16[256,768]{1,0:T(8,128)(2,1)S(1)} %get-tuple-element.55.refs_0_, bf16[768,1280]{1,0:T(8,128)(2,1)S(1)} %get-tuple-element.46.refs_2_.refs_1_, bf16[1280,768]{1,0:T(8,128)(2,1)S(1)} %copy-done.1, bf16[1280,3328]{1,0:T(8,128)(2,1)} %get-tuple-element.54.refs_2_.refs_3_.refs_0_), custom_call_target="tpu_custom_call" | custom-call | flops 10000000000 | bytes 1000 | tf_op jit(solution)/shard_map/backward_ours/pallas_call | solution.py:148
  107.2 8.4 %collective-permute-done.6.refs_4_ = bf16[256,768]{1,0:T(8,128)(2,1)} collective-permute-done((bf16[256,768]{1,0:T(8,128)(2,1)}, bf16[256,768]{1,0:T(8,128)(2,1)}, u32[]{:S(2)}, u32[]{:S(2)}) %collective-permute-start.6) | collective-permute-done | bytes 393248 | tf_op jit(solution)/shard_map/ppermute | solution.py:355
  117.9 10.3 %all-to-all-start.3 = ((bf16[64,8,768]{2,1,0:T(8,128)(2,1)}), bf16[64,8,768]{2,1,0:T(8,128)(2,1)S(1)}, u32[]{:S(2)}, u32[]{:S(2)}) async-start(bf16[64,8,768]{2,1,0:T(8,128)(2,1)} %join_out.1.refs_5_), calls=%async_computation.3 | async-start | bytes 1572864 | tf_op jit(solution)/shard_map/all_to_all | solution.py:362
  128.3 6.1 %backward_near.1 = (bf16[256,768]{1,0:T(8,128)(2,1)S(1)}, bf16[256,768]{1,0:T(8,128)(2,1)S(1)}, bf16[2048,2048]{1,0:T(8,128)(2,1)}) custom-call(bf16[256,768]{1,0:T(8,128)(2,1)S(1)} %collective-permute-done.8.refs_0_, bf16[256,768]{1,0:T(8,128)(2,1)S(1)} %collective-permute-done.9.refs_1_, bf16[768,1280]{1,0:T(8,128)(2,1)} %bitcast.14, ...), custom_call_target="tpu_custom_call" | custom-call | flops 30000001024 | bytes 1000 | tf_op jit(solution)/shard_map/backward_near/pallas_call | solution.py:148
  135.2 10.4 %collective-permute-start.12 = (bf16[256,768]{1,0:T(8,128)(2,1)S(1)}, bf16[256,768]{1,0:T(8,128)(2,1)S(1)}, u32[]{:S(2)}, u32[]{:S(2)}) collective-permute-start(bf16[256,768]{1,0:T(8,128)(2,1)S(1)} %get-tuple-element.64), channel_id=1, source_target_pairs={{0,192},{64,128},{128,64},{192,0},{1,193},{65,129},{129,65},{193,1... | collective-permute-start | bytes 1179656 | tf_op jit(solution)/shard_map/ppermute | solution.py:355
  145.6 4.9 %backward_across.1 = (bf16[256,768]{1,0:T(8,128)(2,1)S(1)}, bf16[2048,2048]{1,0:T(8,128)(2,1)}) custom-call(bf16[256,768]{1,0:T(8,128)(2,1)S(1)} %collective-permute-done.7.refs_0_, bf16[768,1280]{1,0:T(8,128)(2,1)} %bitcast.15, bf16[1280,768]{1,0:T(8,128)(2,1)} %bitcast.18, bf16[1280,3328]{1,0:T(8,128)(2,1)} %get-tuple-element.49.refs_3_.refs_2_, ...), custom_call_target="tpu_custom_call" | custom-call | flops 30000001024 | bytes 1000 | tf_op jit(solution)/shard_map/backward_across/pallas_call | solution.py:148
  153.0 12.1 %collective-permute-done.12.refs_4_ = bf16[256,768]{1,0:T(8,128)(2,1)S(1)} collective-permute-done((bf16[256,768]{1,0:T(8,128)(2,1)S(1)}, bf16[256,768]{1,0:T(8,128)(2,1)S(1)}, u32[]{:S(2)}, u32[]{:S(2)}) %collective-permute-start.12) | collective-permute-done | bytes 393248 | tf_op jit(solution)/shard_map/ppermute | solution.py:355
  166.9 10.4 %all-to-all-start.4 = ((bf16[64,8,768]{2,1,0:T(8,128)(2,1)}), bf16[64,8,768]{2,1,0:T(8,128)(2,1)S(1)}, u32[]{:S(2)}, u32[]{:S(2)}) async-start(bf16[64,8,768]{2,1,0:T(8,128)(2,1)} %join_in.1), calls=%async_computation.4 | async-start | bytes 1572864 | tf_op jit(solution)/shard_map/all_to_all | solution.py:362
  177.3 7.4 %second_grad.1 = (bf16[1280,768]{1,0:T(8,128)(2,1)}, f32[8,128]{1,0:T(8,128)S(1)}) custom-call(bf16[1280,3328]{1,0:T(8,128)(2,1)} %get-tuple-element.54.refs_2_.refs_3_.refs_0_, bf16[1280,3328]{1,0:T(8,128)(2,1)} %get-tuple-element.48.refs_3_.refs_4_.refs_1_, bf16[1280,3328]{1,0:T(8,128)(2,1)} %get-tuple-element.49.refs_3_.refs_2_, ...), custom_call_target="tpu_custom_call" | custom-call | flops 4000000000 | bytes 1000 | tf_op jit(solution)/shard_map/second_grad/pallas_call | solution.py:148
  184.6 8.3 %first_grad.1 = (bf16[768,1280]{1,0:T(8,128)(2,1)}, f32[8,128]{1,0:T(8,128)S(1)}) custom-call(bf16[1280,3328]{1,0:T(8,128)(2,1)} %get-tuple-element.54.refs_2_.refs_3_.refs_0_, bf16[1280,3328]{1,0:T(8,128)(2,1)} %get-tuple-element.48.refs_3_.refs_4_.refs_1_, bf16[1280,3328]{1,0:T(8,128)(2,1)} %get-tuple-element.49.refs_3_.refs_2_, ...), custom_call_target="tpu_custom_call" | custom-call | flops 4000000000 | bytes 1000 | tf_op jit(solution)/shard_map/first_grad/pallas_call | solution.py:148
  195.6 3.7 %all-to-all-done.4 = bf16[64,8,768]{2,1,0:T(8,128)(2,1)S(1)} async-done(((bf16[64,8,768]{2,1,0:T(8,128)(2,1)}), bf16[64,8,768]{2,1,0:T(8,128)(2,1)S(1)}, u32[]{:S(2)}, u32[]{:S(2)}) %all-to-all-start.4) | async-done | bytes 786464 | tf_op jit(solution)/shard_map/all_to_all | solution.py:362
  199.2 3.9 %last.1 = (bf16[7936,512]{1,0:T(8,128)(2,1)}, f32[256,768]{1,0:T(8,128)S(1)}, bf16[256,768]{1,0:T(8,128)(2,1)S(1)}, f32[512,768]{1,0:T(8,128)}) custom-call(s32[2]{0:T(128)S(1)} %pad_add_fusion.refs_0_, bf16[512,768]{1,0:T(8,128)(2,1)S(1)} %bitcast.10, bf16[256,768]{1,0:T(8,128)(2,1)S(1)} %copy-done.8, f32[4096,512]{1,0:T(8,128)} %get-tuple-element.65.refs_3_.refs_0_, ...), custom_call_target="tpu_custom_call" | custom-call | flops 3000000000 | bytes 1000 | tf_op jit(solution)/shard_map/last/pallas_call | solution.py:148
  206.4 7.3 %all-to-all-start.5 = ((bf16[64,4,768]{2,1,0:T(4,128)(2,1)}), bf16[64,4,768]{2,1,0:T(4,128)(2,1)S(1)}, u32[]{:S(2)}, u32[]{:S(2)}) async-start(bf16[64,4,768]{2,1,0:T(4,128)(2,1)} %fold.1), calls=%async_computation.5 | async-start | bytes 786432 | tf_op jit(solution)/shard_map/all_to_all | solution.py:362
  216.5 12.4 %all-to-all-done.5 = bf16[64,4,768]{2,1,0:T(4,128)(2,1)S(1)} async-done(((bf16[64,4,768]{2,1,0:T(4,128)(2,1)}), bf16[64,4,768]{2,1,0:T(4,128)(2,1)S(1)}, u32[]{:S(2)}, u32[]{:S(2)}) %all-to-all-start.5) | async-done | bytes 393248 | tf_op jit(solution)/shard_map/all_to_all | solution.py:362
  230.2 4.1 %collective-permute-done.14 = f32[4,768]{1,0:T(4,128)S(1)} collective-permute-done((f32[4,768]{1,0:T(4,128)S(1)}, f32[4,768]{1,0:T(4,128)S(1)}, u32[]{:S(2)}, u32[]{:S(2)}) %collective-permute-start.14) | collective-permute-done | bytes 12320 | tf_op jit(solution)/shard_map/ppermute | solution.py:351
  (66 shorter events, 42.2 us)
Async XLA Ops:
  0.6 38.8 %copy-start.7 = (bf16[256,768]{1,0:T(8,128)(2,1)S(1)}, bf16[256,768]{1,0:T(8,128)(2,1)}, u32[]{:S(2)}) copy-start(bf16[256,768]{1,0:T(8,128)(2,1)} %refs_2_.3) | copy-start | bytes 1179652
  0.6 38.8 %copy-start.4 = (bf16[256,768]{1,0:T(8,128)(2,1)S(1)}, bf16[256,768]{1,0:T(8,128)(2,1)}, u32[]{:S(2)}) copy-start(bf16[256,768]{1,0:T(8,128)(2,1)} %refs_1_.3) | copy-start | bytes 1179652
  29.0 1.7 collective-permute-start
  34.5 26.9 %all-to-all-start.1 = ((bf16[64,8,768]{2,1,0:T(8,128)(2,1)}), bf16[64,8,768]{2,1,0:T(8,128)(2,1)S(1)}, u32[]{:S(2)}, u32[]{:S(2)}) async-start(bf16[64,8,768]{2,1,0:T(8,128)(2,1)} %bitcast.2), calls=%async_computation.1 | async-start | bytes 1572864 | tf_op jit(solution)/shard_map/all_to_all | solution.py:362
  62.9 15.3 %collective-permute-start.3 = (bf16[256,768]{1,0:T(8,128)(2,1)}, bf16[256,768]{1,0:T(8,128)(2,1)S(1)}, u32[]{:S(2)}, u32[]{:S(2)}) collective-permute-start(bf16[256,768]{1,0:T(8,128)(2,1)} %get-tuple-element.45.after), channel_id=1, source_target_pairs={{0,192},{64,128},{128,64},{192,0},{1,193},{65,129},{129,65},{193,1... | collective-permute-start | bytes 1179656 | tf_op jit(solution)/shard_map/ppermute | solution.py:355
  64.1 14.1 %collective-permute-start.2 = (bf16[256,768]{1,0:T(8,128)(2,1)}, bf16[256,768]{1,0:T(8,128)(2,1)}, u32[]{:S(2)}, u32[]{:S(2)}) collective-permute-start(bf16[256,768]{1,0:T(8,128)(2,1)} %get-tuple-element.45.after), channel_id=1, source_target_pairs={{0,64},{64,0},{128,192},{192,128},{1,65},{65,1},{129,193},{193,129... | collective-permute-start | bytes 1179656 | tf_op jit(solution)/shard_map/ppermute | solution.py:355
  64.4 22.2 %collective-permute-start.1 = (bf16[256,768]{1,0:T(8,128)(2,1)S(1)}, bf16[256,768]{1,0:T(8,128)(2,1)}, u32[]{:S(2)}, u32[]{:S(2)}) collective-permute-start(bf16[256,768]{1,0:T(8,128)(2,1)S(1)} %get-tuple-element.44.refs_0_), channel_id=1, source_target_pairs={{0,128},{64,192},{128,0},{192,64},{1,129},{65,193},{129,1},{193,65... | collective-permute-start | bytes 1179656 | tf_op jit(solution)/shard_map/ppermute | solution.py:355
  67.6 30.1 %all-to-all-start.2 = ((bf16[64,8,768]{2,1,0:T(8,128)(2,1)}), bf16[64,8,768]{2,1,0:T(8,128)(2,1)S(1)}, u32[]{:S(2)}, u32[]{:S(2)}) async-start(bf16[64,8,768]{2,1,0:T(8,128)(2,1)} %bitcast.5), calls=%async_computation.2 | async-start | bytes 1572864 | tf_op jit(solution)/shard_map/all_to_all | solution.py:362
  84.9 21.8 %collective-permute-start.5 = (bf16[256,768]{1,0:T(8,128)(2,1)}, bf16[256,768]{1,0:T(8,128)(2,1)S(1)}, u32[]{:S(2)}, u32[]{:S(2)}) collective-permute-start(bf16[256,768]{1,0:T(8,128)(2,1)} %get-tuple-element.52), channel_id=1, source_target_pairs={{0,64},{64,0},{128,192},{192,128},{1,65},{65,1},{129,193},{193,129... | collective-permute-start | bytes 1179656 | tf_op jit(solution)/shard_map/ppermute | solution.py:355
  85.2 30.3 %collective-permute-start.6 = (bf16[256,768]{1,0:T(8,128)(2,1)}, bf16[256,768]{1,0:T(8,128)(2,1)}, u32[]{:S(2)}, u32[]{:S(2)}) collective-permute-start(bf16[256,768]{1,0:T(8,128)(2,1)} %get-tuple-element.53), channel_id=1, source_target_pairs={{0,192},{64,128},{128,64},{192,0},{1,193},{65,129},{129,65},{193,1... | collective-permute-start | bytes 1179656 | tf_op jit(solution)/shard_map/ppermute | solution.py:355
  91.2 24.4 %collective-permute-start.4 = (bf16[256,768]{1,0:T(8,128)(2,1)}, bf16[256,768]{1,0:T(8,128)(2,1)}, u32[]{:S(2)}, u32[]{:S(2)}) collective-permute-start(bf16[256,768]{1,0:T(8,128)(2,1)} %get-tuple-element.51), channel_id=1, source_target_pairs={{0,128},{64,192},{128,0},{192,64},{1,129},{65,193},{129,1},{193,65... | collective-permute-start | bytes 1179656 | tf_op jit(solution)/shard_map/ppermute | solution.py:355
  99.2 16.4 %copy-start.10 = (f32[256,768]{1,0:T(8,128)S(1)}, f32[256,768]{1,0:T(8,128)}, u32[]{:S(2)}) copy-start(f32[256,768]{1,0:T(8,128)} %copy-done.9) | copy-start | bytes 2359300
  99.2 46.4 %collective-permute-start.7 = (bf16[256,768]{1,0:T(8,128)(2,1)S(1)}, bf16[256,768]{1,0:T(8,128)(2,1)S(1)}, u32[]{:S(2)}, u32[]{:S(2)}) collective-permute-start(bf16[256,768]{1,0:T(8,128)(2,1)S(1)} %get-tuple-element.55.refs_0_), channel_id=1, source_target_pairs={{0,128},{64,192},{128,0},{192,64},{1,129},{65,193},{129,1},{193,65... | collective-permute-start | bytes 1179656 | tf_op jit(solution)/shard_map/ppermute | solution.py:355
  104.5 23.7 %collective-permute-start.9 = (bf16[256,768]{1,0:T(8,128)(2,1)}, bf16[256,768]{1,0:T(8,128)(2,1)S(1)}, u32[]{:S(2)}, u32[]{:S(2)}) collective-permute-start(bf16[256,768]{1,0:T(8,128)(2,1)} %get-tuple-element.60), channel_id=1, source_target_pairs={{0,192},{64,128},{128,64},{192,0},{1,193},{65,129},{129,65},{193,1... | collective-permute-start | bytes 1179656 | tf_op jit(solution)/shard_map/ppermute | solution.py:355
  106.7 21.6 %collective-permute-start.8 = (bf16[256,768]{1,0:T(8,128)(2,1)}, bf16[256,768]{1,0:T(8,128)(2,1)S(1)}, u32[]{:S(2)}, u32[]{:S(2)}) collective-permute-start(bf16[256,768]{1,0:T(8,128)(2,1)} %get-tuple-element.60), channel_id=1, source_target_pairs={{0,64},{64,0},{128,192},{192,128},{1,65},{65,1},{129,193},{193,129... | collective-permute-start | bytes 1179656 | tf_op jit(solution)/shard_map/ppermute | solution.py:355
  117.9 47.2 %all-to-all-start.3 = ((bf16[64,8,768]{2,1,0:T(8,128)(2,1)}), bf16[64,8,768]{2,1,0:T(8,128)(2,1)S(1)}, u32[]{:S(2)}, u32[]{:S(2)}) async-start(bf16[64,8,768]{2,1,0:T(8,128)(2,1)} %join_out.1.refs_5_), calls=%async_computation.3 | async-start | bytes 1572864 | tf_op jit(solution)/shard_map/all_to_all | solution.py:362
  134.5 18.6 %collective-permute-start.11 = (bf16[256,768]{1,0:T(8,128)(2,1)S(1)}, bf16[256,768]{1,0:T(8,128)(2,1)S(1)}, u32[]{:S(2)}, u32[]{:S(2)}) collective-permute-start(bf16[256,768]{1,0:T(8,128)(2,1)S(1)} %get-tuple-element.63), channel_id=1, source_target_pairs={{0,64},{64,0},{128,192},{192,128},{1,65},{65,1},{129,193},{193,129... | collective-permute-start | bytes 1179656 | tf_op jit(solution)/shard_map/ppermute | solution.py:355
  135.2 29.9 %collective-permute-start.12 = (bf16[256,768]{1,0:T(8,128)(2,1)S(1)}, bf16[256,768]{1,0:T(8,128)(2,1)S(1)}, u32[]{:S(2)}, u32[]{:S(2)}) collective-permute-start(bf16[256,768]{1,0:T(8,128)(2,1)S(1)} %get-tuple-element.64), channel_id=1, source_target_pairs={{0,192},{64,128},{128,64},{192,0},{1,193},{65,129},{129,65},{193,1... | collective-permute-start | bytes 1179656 | tf_op jit(solution)/shard_map/ppermute | solution.py:355
  145.6 19.5 %copy-start.12 = (f32[256,768]{1,0:T(8,128)S(1)}, f32[256,768]{1,0:T(8,128)}, u32[]{:S(2)}) copy-start(f32[256,768]{1,0:T(8,128)} %copy-done.11) | copy-start | bytes 2359300
  150.6 14.5 %collective-permute-start.10 = (bf16[256,768]{1,0:T(8,128)(2,1)S(1)}, bf16[256,768]{1,0:T(8,128)(2,1)S(1)}, u32[]{:S(2)}, u32[]{:S(2)}) collective-permute-start(bf16[256,768]{1,0:T(8,128)(2,1)S(1)} %get-tuple-element.62), channel_id=1, source_target_pairs={{0,128},{64,192},{128,0},{192,64},{1,129},{65,193},{129,1},{193,65... | collective-permute-start | bytes 1179656 | tf_op jit(solution)/shard_map/ppermute | solution.py:355
  166.9 32.3 %all-to-all-start.4 = ((bf16[64,8,768]{2,1,0:T(8,128)(2,1)}), bf16[64,8,768]{2,1,0:T(8,128)(2,1)S(1)}, u32[]{:S(2)}, u32[]{:S(2)}) async-start(bf16[64,8,768]{2,1,0:T(8,128)(2,1)} %join_in.1), calls=%async_computation.4 | async-start | bytes 1572864 | tf_op jit(solution)/shard_map/all_to_all | solution.py:362
  203.2 2.4 %collective-permute-start.13 = (bf16[256,768]{1,0:T(8,128)(2,1)S(1)}, bf16[256,768]{1,0:T(8,128)(2,1)S(1)}, u32[]{:S(2)}, u32[]{:S(2)}) collective-permute-start(bf16[256,768]{1,0:T(8,128)(2,1)S(1)} %get-tuple-element.71), channel_id=1, source_target_pairs={{0,1},{1,0},{2,3},{3,2},{4,5},{5,4},{6,7},{7,6},{8,9},{9,8},{10,11... | collective-permute-start | bytes 1179656 | tf_op jit(solution)/shard_map/ppermute | solution.py:351
  206.4 22.5 %all-to-all-start.5 = ((bf16[64,4,768]{2,1,0:T(4,128)(2,1)}), bf16[64,4,768]{2,1,0:T(4,128)(2,1)S(1)}, u32[]{:S(2)}, u32[]{:S(2)}) async-start(bf16[64,4,768]{2,1,0:T(4,128)(2,1)} %fold.1), calls=%async_computation.5 | async-start | bytes 786432 | tf_op jit(solution)/shard_map/all_to_all | solution.py:362
  229.1 5.3 %collective-permute-start.14 = (f32[4,768]{1,0:T(4,128)S(1)}, f32[4,768]{1,0:T(4,128)S(1)}, u32[]{:S(2)}, u32[]{:S(2)}) collective-permute-start(f32[4,768]{1,0:T(4,128)S(1)} %convert_reduce_fusion), channel_id=1, source_target_pairs={{0,128},{128,0},{1,129},{129,1},{2,130},{130,2},{3,131},{131,3},{4... | collective-permute-start | bytes 36872 | tf_op jit(solution)/shard_map/ppermute | solution.py:351
  (9 other events, 38.6 us)
where the time goes:
time: 240 us; the launch traced here: 235 us
  Pallas kernels  68.4 us (29%)
  starting transfers between devices  68.3 us (28%)
  waiting for transfers between devices  62.2 us (26%)
  blocking collectives  27.5 us (11%)
  local copies, waits for them, and re-layouts  6.77 us (3%)
    pallas_call x18, Pallas kernels, call(): pl.pallas_call(run, name=name, out_shape=shapes, in_specs=specs, out_spec...  67.8 us
    all_to_all x5, starting transfers between devices, exchange(): return lax.all_to_all(value, axes, split_axis=0, concat_axis=0, tiled=True)  39.8 us
    all_to_all x5, waiting for transfers between devices, exchange(): return lax.all_to_all(value, axes, split_axis=0, concat_axis=0, tiled=True)  34.7 us
    all_to_all x1, blocking collectives, exchange(): return lax.all_to_all(value, axes, split_axis=0, concat_axis=0, tiled=True)  27.5 us
    ppermute x12, starting transfers between devices, hop(): lax.ppermute(value, ('dp', 'yl'), [(at, at ^ flips) for at in range(4)])  26.3 us
    ppermute x12, waiting for transfers between devices, hop(): lax.ppermute(value, ('dp', 'yl'), [(at, at ^ flips) for at in range(4)])  20.4 us
    ppermute x3, waiting for transfers between devices, swap(): return lax.ppermute(value, axis, [(0, 1), (1, 0)])  7.13 us
    unnamed x26, local copies, waits for them, and re-layouts  5.91 us
  transfers between devices with their start and end apart: 20, of which 8 were waited for; matrix products, arithmetic and copies ran while one was open for 0% of the time, Pallas kernels for 24%

commit v1 on v0

--- a/solution.py
+++ b/solution.py
@@ -95,7 +95,7 @@
         self.rows = max(shape[0], -(-SPARE // width) // 256 * 256 + 256) if room else shape[0]
 
 
-def call(kernel, name, cost, outs, *operands, limit=WIDE):
+def call(kernel, name, cost, outs, *operands, limit=WIDE, extra=()):
     values, specs, scratch, plan, sems = [], [], [], [], 0
 
     def far(shape, dtype, cuts, by_rows, start=0):
@@ -141,7 +141,7 @@
             inner.append(Far(ref, mine[how[0]], mine[-1], *how[1:]))
             if at >= len(values):
                 waiting.append(inner[-1])
-        kernel(*inner)
+        kernel(*inner, *mine[len(scratch) : len(scratch) + len(extra)])
         for one in waiting:
             one.wait()
 
@@ -151,7 +151,7 @@
         out_shape=shapes,
         in_specs=specs,
         out_specs=out_specs,
-        scratch_shapes=scratch + ([pltpu.SemaphoreType.DMA((sems,))] if sems else []),
+        scratch_shapes=scratch + list(extra) + ([pltpu.SemaphoreType.DMA((sems,))] if sems else []),
         compiler_params=pltpu.CompilerParams(vmem_limit_bytes=limit),
         cost_estimate=pl.CostEstimate(flops=cost * MICRO, bytes_accessed=1000, transcendentals=0),
     )(*values)
@@ -225,34 +225,26 @@
             far.copy(step, False).wait()
 
 
-def load(first, second, first_here, second_here, sems):
-    copies = [
-        pltpu.make_async_copy(first, first_here, sems.at[0]),
-        pltpu.make_async_copy(second, second_here, sems.at[1]),
-    ]
-    for copy in copies:
-        copy.start()
-    for copy in copies:
-        copy.wait()
-
-
 def forward(*refs):
     blocks = (len(refs) - 3) // 2
     low, first, second, outs, acts = refs[:blocks], *refs[blocks : blocks + 2], refs[-blocks - 1 : -1], refs[-1]
+    begin(first, second)
     here = jnp.concatenate([ref[...] for ref in low], axis=0)
     acts.put(here, 0)
     total = None
-    for step in range(first.shape[1] // TILE):
+    for step in range(first.here.shape[1] // TILE):
+        arrived(step, first)
         part = slice(step * TILE, step * TILE + TILE)
-        value = dot(here, first[:, part])
+        value = dot(here, first.here[:, part])
         square = value * value
         bend = jnp.tanh(ROOT * value * (1.0 + CUBIC * square))
         gate = 0.5 + 0.5 * bend
         active = (value * gate).astype(BF)
         acts.put(active, 1 + step)
         rise = (0.5 * ROOT) * value * (1.0 - bend * bend) * (1.0 + (3.0 * CUBIC) * square)
-        acts.put((gate + rise).astype(BF), 1 + first.shape[1] // TILE + step)
-        term = dot(active, second[part, :])
+        acts.put((gate + rise).astype(BF), 1 + first.here.shape[1] // TILE + step)
+        arrived(step, second)
+        term = dot(active, second.here[part, :])
         total = term if total is None else total + term
     for at, out in enumerate(outs):
         out[...] = total[at * 256 : at * 256 + 256].astype(out.dtype)
@@ -263,18 +255,17 @@
     low, first, second, slope, outs, kept = (
         refs[:blocks], *refs[blocks : blocks + 3], refs[-blocks - 1 : -1], refs[-1],
     )
-    far = [one for one in (second, slope, first) if isinstance(one, Far)]
-    begin(*far)
-    first, second = (one.here if isinstance(one, Far) else one for one in (first, second))
+    begin(second, slope, first)
     here = jnp.concatenate([ref[...] for ref in low], axis=0)
     kept.put(here, 0)
     total = None
-    for step in range(first.shape[1] // TILE):
-        arrived(step, *far)
+    for step in range(first.here.shape[1] // TILE):
+        arrived(step, second, slope)
         part = slice(step * TILE, step * TILE + TILE)
-        rounded = (dot_last(here, second[part, :]) * slope.here[:, part].astype(F32)).astype(BF)
+        rounded = (dot_last(here, second.here[part, :]) * slope.here[:, part].astype(F32)).astype(BF)
         kept.put(rounded, 1 + step)
-        term = dot_last(rounded, first[:, part])
+        arrived(step, first)
+        term = dot_last(rounded, first.here[:, part])
         total = term if total is None else total + term
     for at, out in enumerate(outs):
         out[...] = total[at * 256 : at * 256 + 256].astype(out.dtype)
@@ -389,18 +380,6 @@
     def inward(routed, *after):
         return call(part_ways, "part_ways", 1, [block, block], place, routed, *after)
 
-    def weights(after):
-        return pl.pallas_call(
-            lambda first, second, after, *refs: load(first, second, *refs),
-            name="load",
-            out_shape=[jax.ShapeDtypeStruct(value.shape, BF) for value in (first, second)],
-            in_specs=[THERE] * 3,
-            out_specs=[HERE] * 2,
-            scratch_shapes=[pltpu.SemaphoreType.DMA((2,))],
-            compiler_params=pltpu.CompilerParams(vmem_limit_bytes=WIDE),
-            cost_estimate=pl.CostEstimate(flops=1000, bytes_accessed=1000, transcendentals=0),
-        )(first, second, after)
-
     act_cuts, kept_cuts = [(0, D)], [(0, D)]
     for step in range(2 * steps):
         act_cuts += [(D + TILE * step, D + TILE * (step + 1))]
@@ -412,24 +391,22 @@
     def ahead(name, blocks, outs, *after):
         rows = 256 * len(blocks)
         acts = Out((rows, D + 2 * half), BF, act_cuts, room=True)
-        return call(forward, name, 60 if name == "forward_across" else 0, outs + [acts], *blocks, *here, *after, limit=WIDE)
-
-    def back(name, blocks, outs, weights, acts, *after):
+        return call(forward, name, 60 if name == "forward_across" else 0, outs + [acts], *blocks, *fetched, *after, limit=TIGHT)
+
+    def back(name, blocks, outs, acts, *after):
         rows = 256 * len(blocks)
         kept = Out((rows, D + half), BF, kept_cuts, room=True)
         slope = In(acts, rows, pieces, start=slope_at, width=half)
-        cost, limit = (10, WIDE) if weights is here else (30, TIGHT)
-        return call(backward, name, cost, outs + [kept], *blocks, *weights, slope, *after, limit=limit)
-
-    def join_up(name, ours, across, near, around, *after):
-        (out,) = call(
-            join, name, 20, [((64, 2 * SLOTS, D), BF)],
-            place, ours, hop(across, ACROSS), hop(near, NEXT), hop(around, AROUND), *after,
-        )
-        return out
+        cost = 10 if name == "backward_ours" else 30
+        return call(backward, name, cost, outs + [kept], *blocks, *fetched, slope, *after, limit=TIGHT)
+
+    def outward(across, near, around):
+        return hop(across, ACROSS), hop(near, NEXT), hop(around, AROUND)
+
+    def join_up(name, *operands):
+        return call(join, name, 20, [((64, 2 * SLOTS, D), BF)], place, *operands)[0]
 
     ours, theirs = inward(rows, After(early))
-    here = weights(theirs)
     near_out, around_out, acts_near = ahead(
         "forward_near", [hop(theirs, NEXT), hop(theirs, AROUND)], [block, block]
     )
@@ -439,17 +416,19 @@
     ours_out, acts_ours = ahead("forward_ours", [ours], [final], After(acts_across))
 
     ours, theirs = inward(grads, After(acts_ours))
+    ours_in, kept_ours = back("backward_ours", [ours], [final], acts_ours)
+    received = outward(across_out, near_out, around_out)
+    ours, theirs, *received = lax.optimization_barrier((ours, theirs, *received))
     near, around, across = hop(theirs, NEXT), hop(theirs, AROUND), hop(ours, ACROSS)
-    ours_in, kept_ours = back("backward_ours", [ours], [final], here, acts_ours)
-    out = join_up("join_out", ours_out, across_out, near_out, around_out, After(kept_ours))
+    out = join_up("join_out", ours_out, *received, After(kept_ours))
     slot_output = route(out).reshape(512, D)
     near_in, around_in, kept_near = back(
-        "backward_near", [near, around], [block, block], fetched, acts_near, After(out)
+        "backward_near", [near, around], [block, block], acts_near, After(out)
     )
     across_in, kept_across = back(
-        "backward_across", [across], [block], fetched, acts_across, After(kept_near)
-    )
-    into = join_up("join_in", ours_in, across_in, near_in, around_in, After(slot_output))
+        "backward_across", [across], [block], acts_across, After(kept_near)
+    )
+    into = join_up("join_in", ours_in, *outward(across_in, near_in, around_in), After(slot_output))
     slot_in_grad = route(into).reshape(512, D)
 
     def weight_sum(name, towards, shape):
@@ -466,10 +445,10 @@
     layer_out, mix = call(
         middle, "middle", 2, [Out(*block), share], slot_output, In(out_grad), In(combine, 256)
     )
-    score_grad, kept, sent, _ = call(
-        last, "last", 3, [Out((256, 512), BF, room=True), final, block, ((512, D), F32)],
+    score_grad, kept, sent = call(
+        last, "last", 3, [Out((256, 512), BF, room=True), final, block],
         place, slot_in_grad, In(patches), In(dispatch, 256), In(mix, 256),
-        After(first_done), After(second_done),
+        After(first_done), After(second_done), extra=(pltpu.VMEM((512, D), F32),),
     )
     (folded,) = call(fold, "fold", 1, [((64, SLOTS, D), BF)], kept, swap(sent, "core"))
     own_total = jnp.sum(exchange(folded, PLANE).astype(F32), axis=0)

time: 240 us -> 229 us (0.954)
  waiting for transfers between devices: 62.2 us -> 55.6 us
  local copies, waits for them, and re-layouts: 6.77 us -> 2.77 us
    ppermute x12, waiting for transfers between devices: 20.4 us -> 14 us  [hop(): lax.ppermute(value, ('dp', 'yl'), [(at, at ^ flips) for at in range(4)])]
    unnamed x26 -> x14, local copies, waits for them, and re-layouts: 5.91 us -> 1.9 us
  transfers between devices with their start and end apart: 20 -> 20, of which waited for: 8 -> 9; matrix products, arithmetic and copies ran while one was open for 0% -> 0% of each run, Pallas kernels for 24% -> 27%
where the time goes in v1:
time: 229 us; the launch traced here: 225 us
  Pallas kernels  68.9 us (30%)
  starting transfers between devices  68.1 us (30%)
  waiting for transfers between devices  55.6 us (24%)
  blocking collectives  27.5 us (12%)
  local copies, waits for them, and re-layouts  2.77 us (1%)
    pallas_call x18, Pallas kernels, call(): pl.pallas_call(run, name=name, out_shape=shapes, in_specs=specs, out_spec...  68.9 us
    all_to_all x5, starting transfers between devices, exchange(): return lax.all_to_all(value, axes, split_axis=0, concat_axis=0, tiled=True)  38 us
    all_to_all x5, waiting for transfers between devices, exchange(): return lax.all_to_all(value, axes, split_axis=0, concat_axis=0, tiled=True)  34.6 us
    ppermute x12, starting transfers between devices, hop(): lax.ppermute(value, ('dp', 'yl'), [(at, at ^ flips) for at in range(4)])  27.7 us
    all_to_all x1, blocking collectives, exchange(): return lax.all_to_all(value, axes, split_axis=0, concat_axis=0, tiled=True)  27.5 us
    ppermute x12, waiting for transfers between devices, hop(): lax.ppermute(value, ('dp', 'yl'), [(at, at ^ flips) for at in range(4)])  14 us
    ppermute x3, waiting for transfers between devices, swap(): return lax.ppermute(value, axis, [(0, 1), (1, 0)])  6.94 us
  transfers between devices with their start and end apart: 20, of which 9 were waited for; matrix products, arithmetic and copies ran while one was open for 0% of the time, Pallas kernels for 27%

profile of v1, /device:TPU:24, one launch (start us, length us, event | category | flops | bytes accessed | tf_op | source)
XLA Modules:
  0.0 224.7 jit_solution(15072015941698657374)
XLA Ops:
  1.5 27.5 %all_to_all.30.refs_2_ = bf16[64,4,768]{2,1,0:T(4,128)(2,1)S(1)} all-to-all(bf16[64,4,768]{2,1,0:T(4,128)(2,1)S(1)} %broadcast_in_dim.12), channel_id=1, replica_groups=mesh['dp'=2,'yl'=2,'z'=8,'x'=4,'core'=2] {'z','x','yl'}, dimensions={0} | all-to-all | bytes 786432 | tf_op jit(solution)/shard_map/all_to_all | solution.py:353
  31.7 2.8 %front.1 = (bf16[512,768]{1,0:T(8,128)(2,1)}, f32[4096,512]{1,0:T(8,128)}, bf16[5376,768]{1,0:T(8,128)(2,1)}) custom-call(s32[2]{0:T(128)S(1)} %pad_add_fusion.refs_0_, bf16[256,768]{1,0:T(8,128)(2,1)S(1)} %copy-done.2, bf16[64,4,768]{2,1,0:T(4,128)(2,1)S(1)} %all_to_all.30.refs_2_, bf16[64,4,768]{2,1,0:T(4,128)(2,1)S(1)} %collective-permute-done.refs_3_), custom_call_target="tpu_custom_call" | custom-call | flops 3000000000 | bytes 1000 | tf_op jit(solution)/shard_map/front/pallas_call | solution.py:148
  34.5 5.0 %all-to-all-start.1 = ((bf16[64,8,768]{2,1,0:T(8,128)(2,1)}), bf16[64,8,768]{2,1,0:T(8,128)(2,1)S(1)}, u32[]{:S(2)}, u32[]{:S(2)}) async-start(bf16[64,8,768]{2,1,0:T(8,128)(2,1)} %bitcast.2), calls=%async_computation.1 | async-start | bytes 1572864 | tf_op jit(solution)/shard_map/all_to_all | solution.py:353
  39.5 3.3 %front_grads.1 = (bf16[512,768]{1,0:T(8,128)(2,1)}, f32[4096,512]{1,0:T(8,128)}) custom-call(bf16[256,768]{1,0:T(8,128)(2,1)S(1)} %copy-done.3, bf16[5376,768]{1,0:T(8,128)(2,1)} %get-tuple-element.45.refs_1_.refs_3_, bf16[256,768]{1,0:T(8,128)(2,1)S(1)} %copy-done), custom_call_target="tpu_custom_call" | custom-call | flops 2000000000 | bytes 1000 | tf_op jit(solution)/shard_map/front_grads/pallas_call | solution.py:148
  42.8 18.6 %all-to-all-done.1.refs_1_ = bf16[64,8,768]{2,1,0:T(8,128)(2,1)S(1)} async-done(((bf16[64,8,768]{2,1,0:T(8,128)(2,1)}), bf16[64,8,768]{2,1,0:T(8,128)(2,1)S(1)}, u32[]{:S(2)}, u32[]{:S(2)}) %all-to-all-start.1) | async-done | bytes 786464 | tf_op jit(solution)/shard_map/all_to_all | solution.py:353
  63.9 3.1 %collective-permute-start.1 = (bf16[256,768]{1,0:T(8,128)(2,1)S(1)}, bf16[256,768]{1,0:T(8,128)(2,1)S(1)}, u32[]{:S(2)}, u32[]{:S(2)}) collective-permute-start(bf16[256,768]{1,0:T(8,128)(2,1)S(1)} %get-tuple-element.47.refs_0_), channel_id=1, source_target_pairs={{0,128},{64,192},{128,0},{192,64},{1,129},{65,193},{129,1},{193,65... | collective-permute-start | bytes 1179656 | tf_op jit(solution)/shard_map/ppermute | solution.py:346
  67.0 6.9 %all-to-all-start.2 = ((bf16[64,8,768]{2,1,0:T(8,128)(2,1)}), bf16[64,8,768]{2,1,0:T(8,128)(2,1)S(1)}, u32[]{:S(2)}, u32[]{:S(2)}) async-start(bf16[64,8,768]{2,1,0:T(8,128)(2,1)} %bitcast.5), calls=%async_computation.2 | async-start | bytes 1572864 | tf_op jit(solution)/shard_map/all_to_all | solution.py:353
  75.5 7.1 %forward_near.1 = (bf16[256,768]{1,0:T(8,128)(2,1)}, bf16[256,768]{1,0:T(8,128)(2,1)S(1)}, bf16[1280,3328]{1,0:T(8,128)(2,1)}) custom-call(bf16[256,768]{1,0:T(8,128)(2,1)S(1)} %collective-permute-done.2.refs_0_, bf16[256,768]{1,0:T(8,128)(2,1)S(1)} %collective-permute-done.3.refs_1_, bf16[768,1280]{1,0:T(8,128)(2,1)} %bitcast.14, bf16[1280,768]{1,0:T(8,128)(2,1)} %bitcast.20), custom_call_target="tpu_custom_call" | custom-call | bytes 1000 | tf_op jit(solution)/shard_map/forward_near/pallas_call | solution.py:148
  83.0 2.8 %collective-permute-start.6 = (bf16[256,768]{1,0:T(8,128)(2,1)S(1)}, bf16[256,768]{1,0:T(8,128)(2,1)S(1)}, u32[]{:S(2)}, u32[]{:S(2)}) collective-permute-start(bf16[256,768]{1,0:T(8,128)(2,1)S(1)} %get-tuple-element.57), channel_id=1, source_target_pairs={{0,192},{64,128},{128,64},{192,0},{1,193},{65,129},{129,65},{193,1... | collective-permute-start | bytes 1179656 | tf_op jit(solution)/shard_map/ppermute | solution.py:346
  85.8 5.4 %forward_across.1 = (bf16[256,768]{1,0:T(8,128)(2,1)}, bf16[1280,3328]{1,0:T(8,128)(2,1)}) custom-call(bf16[256,768]{1,0:T(8,128)(2,1)S(1)} %collective-permute-done.1.refs_0_, bf16[768,1280]{1,0:T(8,128)(2,1)} %bitcast.15, bf16[1280,768]{1,0:T(8,128)(2,1)} %bitcast.21, bf16[1280,3328]{1,0:T(8,128)(2,1)} %get-tuple-element.49.refs_3_.refs_4_.refs_1_), custom_call_target="tpu_custom_call" | custom-call | flops 60000002048 | bytes 1000 | tf_op jit(solution)/shard_map/forward_across/pallas_call | solution.py:148
  92.5 4.6 %forward_ours.1 = (f32[256,768]{1,0:T(8,128)S(1)}, bf16[1280,3328]{1,0:T(8,128)(2,1)}) custom-call(bf16[256,768]{1,0:T(8,128)(2,1)S(1)} %get-tuple-element.47.refs_0_, bf16[768,1280]{1,0:T(8,128)(2,1)} %bitcast.16, bf16[1280,768]{1,0:T(8,128)(2,1)} %bitcast.22, bf16[1280,3328]{1,0:T(8,128)(2,1)} %get-tuple-element.50.refs_3_.refs_2_), custom_call_target="tpu_custom_call" | custom-call | bytes 1000 | tf_op jit(solution)/shard_map/forward_ours/pallas_call | solution.py:148
  98.6 4.6 %backward_ours.1 = (f32[256,768]{1,0:T(8,128)S(1)}, bf16[2048,2048]{1,0:T(8,128)(2,1)}) custom-call(bf16[256,768]{1,0:T(8,128)(2,1)S(1)} %get-tuple-element.65.refs_0_, bf16[768,1280]{1,0:T(8,128)(2,1)} %bitcast.17, bf16[1280,768]{1,0:T(8,128)(2,1)} %bitcast.23, bf16[1280,3328]{1,0:T(8,128)(2,1)} %get-tuple-element.52.refs_2_.refs_3_.refs_0_), custom_call_target="tpu_custom_call" | custom-call | flops 10000000000 | bytes 1000 | tf_op jit(solution)/shard_map/backward_ours/pallas_call | solution.py:148
  110.8 8.5 %all-to-all-start.3 = ((bf16[64,8,768]{2,1,0:T(8,128)(2,1)}), bf16[64,8,768]{2,1,0:T(8,128)(2,1)S(1)}, u32[]{:S(2)}, u32[]{:S(2)}) async-start(bf16[64,8,768]{2,1,0:T(8,128)(2,1)} %join_out.1.refs_5_), calls=%async_computation.3 | async-start | bytes 1572864 | tf_op jit(solution)/shard_map/all_to_all | solution.py:353
  119.3 5.9 %backward_near.1 = (bf16[256,768]{1,0:T(8,128)(2,1)S(1)}, bf16[256,768]{1,0:T(8,128)(2,1)S(1)}, bf16[2048,2048]{1,0:T(8,128)(2,1)}) custom-call(bf16[256,768]{1,0:T(8,128)(2,1)S(1)} %collective-permute-done.8.refs_0_, bf16[256,768]{1,0:T(8,128)(2,1)S(1)} %collective-permute-done.9.refs_1_, bf16[768,1280]{1,0:T(8,128)(2,1)} %bitcast.18, ...), custom_call_target="tpu_custom_call" | custom-call | flops 30000001024 | bytes 1000 | tf_op jit(solution)/shard_map/backward_near/pallas_call | solution.py:148
  125.3 11.0 %collective-permute-start.12 = (bf16[256,768]{1,0:T(8,128)(2,1)S(1)}, bf16[256,768]{1,0:T(8,128)(2,1)S(1)}, u32[]{:S(2)}, u32[]{:S(2)}) collective-permute-start(bf16[256,768]{1,0:T(8,128)(2,1)S(1)} %get-tuple-element.70), channel_id=1, source_target_pairs={{0,192},{64,128},{128,64},{192,0},{1,193},{65,129},{129,65},{193,1... | collective-permute-start | bytes 1179656 | tf_op jit(solution)/shard_map/ppermute | solution.py:346
  136.3 4.7 %backward_across.1 = (bf16[256,768]{1,0:T(8,128)(2,1)S(1)}, bf16[2048,2048]{1,0:T(8,128)(2,1)}) custom-call(bf16[256,768]{1,0:T(8,128)(2,1)S(1)} %collective-permute-done.7.refs_0_, bf16[768,1280]{1,0:T(8,128)(2,1)} %bitcast.19, bf16[1280,768]{1,0:T(8,128)(2,1)} %bitcast.25, bf16[1280,3328]{1,0:T(8,128)(2,1)} %get-tuple-element.50.refs_3_.refs_2_, ...), custom_call_target="tpu_custom_call" | custom-call | flops 30000001024 | bytes 1000 | tf_op jit(solution)/shard_map/backward_across/pallas_call | solution.py:148
  143.6 12.3 %collective-permute-done.12.refs_4_ = bf16[256,768]{1,0:T(8,128)(2,1)S(1)} collective-permute-done((bf16[256,768]{1,0:T(8,128)(2,1)S(1)}, bf16[256,768]{1,0:T(8,128)(2,1)S(1)}, u32[]{:S(2)}, u32[]{:S(2)}) %collective-permute-start.12) | collective-permute-done | bytes 393248 | tf_op jit(solution)/shard_map/ppermute | solution.py:346
  157.7 10.4 %all-to-all-start.4 = ((bf16[64,8,768]{2,1,0:T(8,128)(2,1)}), bf16[64,8,768]{2,1,0:T(8,128)(2,1)S(1)}, u32[]{:S(2)}, u32[]{:S(2)}) async-start(bf16[64,8,768]{2,1,0:T(8,128)(2,1)} %join_in.1), calls=%async_computation.4 | async-start | bytes 1572864 | tf_op jit(solution)/shard_map/all_to_all | solution.py:353
  168.0 7.4 %second_grad.1 = (bf16[1280,768]{1,0:T(8,128)(2,1)}, f32[8,128]{1,0:T(8,128)S(1)}) custom-call(bf16[1280,3328]{1,0:T(8,128)(2,1)} %get-tuple-element.52.refs_2_.refs_3_.refs_0_, bf16[1280,3328]{1,0:T(8,128)(2,1)} %get-tuple-element.49.refs_3_.refs_4_.refs_1_, bf16[1280,3328]{1,0:T(8,128)(2,1)} %get-tuple-element.50.refs_3_.refs_2_, ...), custom_call_target="tpu_custom_call" | custom-call | flops 4000000000 | bytes 1000 | tf_op jit(solution)/shard_map/second_grad/pallas_call | solution.py:148
  175.4 8.3 %first_grad.1 = (bf16[768,1280]{1,0:T(8,128)(2,1)}, f32[8,128]{1,0:T(8,128)S(1)}) custom-call(bf16[1280,3328]{1,0:T(8,128)(2,1)} %get-tuple-element.52.refs_2_.refs_3_.refs_0_, bf16[1280,3328]{1,0:T(8,128)(2,1)} %get-tuple-element.49.refs_3_.refs_4_.refs_1_, bf16[1280,3328]{1,0:T(8,128)(2,1)} %get-tuple-element.50.refs_3_.refs_2_, ...), custom_call_target="tpu_custom_call" | custom-call | flops 4000000000 | bytes 1000 | tf_op jit(solution)/shard_map/first_grad/pallas_call | solution.py:148
  186.3 3.7 %all-to-all-done.4 = bf16[64,8,768]{2,1,0:T(8,128)(2,1)S(1)} async-done(((bf16[64,8,768]{2,1,0:T(8,128)(2,1)}), bf16[64,8,768]{2,1,0:T(8,128)(2,1)S(1)}, u32[]{:S(2)}, u32[]{:S(2)}) %all-to-all-start.4) | async-done | bytes 786464 | tf_op jit(solution)/shard_map/all_to_all | solution.py:353
  196.0 7.3 %all-to-all-start.5 = ((bf16[64,4,768]{2,1,0:T(4,128)(2,1)}), bf16[64,4,768]{2,1,0:T(4,128)(2,1)S(1)}, u32[]{:S(2)}, u32[]{:S(2)}) async-start(bf16[64,4,768]{2,1,0:T(4,128)(2,1)} %fold.1), calls=%async_computation.5 | async-start | bytes 786432 | tf_op jit(solution)/shard_map/all_to_all | solution.py:353
  206.1 12.4 %all-to-all-done.5 = bf16[64,4,768]{2,1,0:T(4,128)(2,1)S(1)} async-done(((bf16[64,4,768]{2,1,0:T(4,128)(2,1)}), bf16[64,4,768]{2,1,0:T(4,128)(2,1)S(1)}, u32[]{:S(2)}, u32[]{:S(2)}) %all-to-all-start.5) | async-done | bytes 393248 | tf_op jit(solution)/shard_map/all_to_all | solution.py:353
  220.0 3.9 %collective-permute-done.14 = f32[4,768]{1,0:T(4,128)S(1)} collective-permute-done((f32[4,768]{1,0:T(4,128)S(1)}, f32[4,768]{1,0:T(4,128)S(1)}, u32[]{:S(2)}, u32[]{:S(2)}) %collective-permute-start.14) | collective-permute-done | bytes 12320 | tf_op jit(solution)/shard_map/ppermute | solution.py:342
  (53 shorter events, 36.3 us)
Async XLA Ops:
  0.6 38.8 %copy-start.3 = (bf16[256,768]{1,0:T(8,128)(2,1)S(1)}, bf16[256,768]{1,0:T(8,128)(2,1)}, u32[]{:S(2)}) copy-start(bf16[256,768]{1,0:T(8,128)(2,1)} %refs_2_.3) | copy-start | bytes 1179652
  0.6 38.8 %copy-start = (bf16[256,768]{1,0:T(8,128)(2,1)S(1)}, bf16[256,768]{1,0:T(8,128)(2,1)}, u32[]{:S(2)}) copy-start(bf16[256,768]{1,0:T(8,128)(2,1)} %refs_1_.3) | copy-start | bytes 1179652
  29.0 1.7 collective-permute-start
  34.5 26.9 %all-to-all-start.1 = ((bf16[64,8,768]{2,1,0:T(8,128)(2,1)}), bf16[64,8,768]{2,1,0:T(8,128)(2,1)S(1)}, u32[]{:S(2)}, u32[]{:S(2)}) async-start(bf16[64,8,768]{2,1,0:T(8,128)(2,1)} %bitcast.2), calls=%async_computation.1 | async-start | bytes 1572864 | tf_op jit(solution)/shard_map/all_to_all | solution.py:353
  62.2 13.2 %collective-permute-start.3 = (bf16[256,768]{1,0:T(8,128)(2,1)S(1)}, bf16[256,768]{1,0:T(8,128)(2,1)S(1)}, u32[]{:S(2)}, u32[]{:S(2)}) collective-permute-start(bf16[256,768]{1,0:T(8,128)(2,1)S(1)} %get-tuple-element.48), channel_id=1, source_target_pairs={{0,192},{64,128},{128,64},{192,0},{1,193},{65,129},{129,65},{193,1... | collective-permute-start | bytes 1179656 | tf_op jit(solution)/shard_map/ppermute | solution.py:346
  63.5 12.0 %collective-permute-start.2 = (bf16[256,768]{1,0:T(8,128)(2,1)S(1)}, bf16[256,768]{1,0:T(8,128)(2,1)S(1)}, u32[]{:S(2)}, u32[]{:S(2)}) collective-permute-start(bf16[256,768]{1,0:T(8,128)(2,1)S(1)} %get-tuple-element.48), channel_id=1, source_target_pairs={{0,64},{64,0},{128,192},{192,128},{1,65},{65,1},{129,193},{193,129... | collective-permute-start | bytes 1179656 | tf_op jit(solution)/shard_map/ppermute | solution.py:346
  63.9 21.9 %collective-permute-start.1 = (bf16[256,768]{1,0:T(8,128)(2,1)S(1)}, bf16[256,768]{1,0:T(8,128)(2,1)S(1)}, u32[]{:S(2)}, u32[]{:S(2)}) collective-permute-start(bf16[256,768]{1,0:T(8,128)(2,1)S(1)} %get-tuple-element.47.refs_0_), channel_id=1, source_target_pairs={{0,128},{64,192},{128,0},{192,64},{1,129},{65,193},{129,1},{193,65... | collective-permute-start | bytes 1179656 | tf_op jit(solution)/shard_map/ppermute | solution.py:346
  67.0 30.2 %all-to-all-start.2 = ((bf16[64,8,768]{2,1,0:T(8,128)(2,1)}), bf16[64,8,768]{2,1,0:T(8,128)(2,1)S(1)}, u32[]{:S(2)}, u32[]{:S(2)}) async-start(bf16[64,8,768]{2,1,0:T(8,128)(2,1)} %bitcast.5), calls=%async_computation.2 | async-start | bytes 1572864 | tf_op jit(solution)/shard_map/all_to_all | solution.py:353
  82.6 21.5 %collective-permute-start.5 = (bf16[256,768]{1,0:T(8,128)(2,1)}, bf16[256,768]{1,0:T(8,128)(2,1)S(1)}, u32[]{:S(2)}, u32[]{:S(2)}) collective-permute-start(bf16[256,768]{1,0:T(8,128)(2,1)} %get-tuple-element.56), channel_id=1, source_target_pairs={{0,64},{64,0},{128,192},{192,128},{1,65},{65,1},{129,193},{193,129... | collective-permute-start | bytes 1179656 | tf_op jit(solution)/shard_map/ppermute | solution.py:346
  83.0 21.1 %collective-permute-start.6 = (bf16[256,768]{1,0:T(8,128)(2,1)S(1)}, bf16[256,768]{1,0:T(8,128)(2,1)S(1)}, u32[]{:S(2)}, u32[]{:S(2)}) collective-permute-start(bf16[256,768]{1,0:T(8,128)(2,1)S(1)} %get-tuple-element.57), channel_id=1, source_target_pairs={{0,192},{64,128},{128,64},{192,0},{1,193},{65,129},{129,65},{193,1... | collective-permute-start | bytes 1179656 | tf_op jit(solution)/shard_map/ppermute | solution.py:346
  91.2 13.0 %collective-permute-start.4 = (bf16[256,768]{1,0:T(8,128)(2,1)}, bf16[256,768]{1,0:T(8,128)(2,1)S(1)}, u32[]{:S(2)}, u32[]{:S(2)}) collective-permute-start(bf16[256,768]{1,0:T(8,128)(2,1)} %get-tuple-element.55), channel_id=1, source_target_pairs={{0,128},{64,192},{128,0},{192,64},{1,129},{65,193},{129,1},{193,65... | collective-permute-start | bytes 1179656 | tf_op jit(solution)/shard_map/ppermute | solution.py:346
  104.2 15.1 %collective-permute-start.9 = (bf16[256,768]{1,0:T(8,128)(2,1)}, bf16[256,768]{1,0:T(8,128)(2,1)S(1)}, u32[]{:S(2)}, u32[]{:S(2)}) collective-permute-start(bf16[256,768]{1,0:T(8,128)(2,1)} %get-tuple-element.66), channel_id=1, source_target_pairs={{0,192},{64,128},{128,64},{192,0},{1,193},{65,129},{129,65},{193,1... | collective-permute-start | bytes 1179656 | tf_op jit(solution)/shard_map/ppermute | solution.py:346
  106.3 13.1 %collective-permute-start.8 = (bf16[256,768]{1,0:T(8,128)(2,1)}, bf16[256,768]{1,0:T(8,128)(2,1)S(1)}, u32[]{:S(2)}, u32[]{:S(2)}) collective-permute-start(bf16[256,768]{1,0:T(8,128)(2,1)} %get-tuple-element.66), channel_id=1, source_target_pairs={{0,64},{64,0},{128,192},{192,128},{1,65},{65,1},{129,193},{193,129... | collective-permute-start | bytes 1179656 | tf_op jit(solution)/shard_map/ppermute | solution.py:346
  106.5 29.8 %collective-permute-start.7 = (bf16[256,768]{1,0:T(8,128)(2,1)S(1)}, bf16[256,768]{1,0:T(8,128)(2,1)S(1)}, u32[]{:S(2)}, u32[]{:S(2)}) collective-permute-start(bf16[256,768]{1,0:T(8,128)(2,1)S(1)} %get-tuple-element.65.refs_0_), channel_id=1, source_target_pairs={{0,128},{64,192},{128,0},{192,64},{1,129},{65,193},{129,1},{193,65... | collective-permute-start | bytes 1179656 | tf_op jit(solution)/shard_map/ppermute | solution.py:346
  110.8 45.1 %all-to-all-start.3 = ((bf16[64,8,768]{2,1,0:T(8,128)(2,1)}), bf16[64,8,768]{2,1,0:T(8,128)(2,1)S(1)}, u32[]{:S(2)}, u32[]{:S(2)}) async-start(bf16[64,8,768]{2,1,0:T(8,128)(2,1)} %join_out.1.refs_5_), calls=%async_computation.3 | async-start | bytes 1572864 | tf_op jit(solution)/shard_map/all_to_all | solution.py:353
  125.2 18.4 %collective-permute-start.11 = (bf16[256,768]{1,0:T(8,128)(2,1)S(1)}, bf16[256,768]{1,0:T(8,128)(2,1)S(1)}, u32[]{:S(2)}, u32[]{:S(2)}) collective-permute-start(bf16[256,768]{1,0:T(8,128)(2,1)S(1)} %get-tuple-element.69), channel_id=1, source_target_pairs={{0,64},{64,0},{128,192},{192,128},{1,65},{65,1},{129,193},{193,129... | collective-permute-start | bytes 1179656 | tf_op jit(solution)/shard_map/ppermute | solution.py:346
  125.3 30.5 %collective-permute-start.12 = (bf16[256,768]{1,0:T(8,128)(2,1)S(1)}, bf16[256,768]{1,0:T(8,128)(2,1)S(1)}, u32[]{:S(2)}, u32[]{:S(2)}) collective-permute-start(bf16[256,768]{1,0:T(8,128)(2,1)S(1)} %get-tuple-element.70), channel_id=1, source_target_pairs={{0,192},{64,128},{128,64},{192,0},{1,193},{65,129},{129,65},{193,1... | collective-permute-start | bytes 1179656 | tf_op jit(solution)/shard_map/ppermute | solution.py:346
  136.3 19.6 %copy-start.6 = (f32[256,768]{1,0:T(8,128)S(1)}, f32[256,768]{1,0:T(8,128)}, u32[]{:S(2)}) copy-start(f32[256,768]{1,0:T(8,128)} %copy-done.5) | copy-start | bytes 2359300
  141.0 14.9 %collective-permute-start.10 = (bf16[256,768]{1,0:T(8,128)(2,1)S(1)}, bf16[256,768]{1,0:T(8,128)(2,1)S(1)}, u32[]{:S(2)}, u32[]{:S(2)}) collective-permute-start(bf16[256,768]{1,0:T(8,128)(2,1)S(1)} %get-tuple-element.68), channel_id=1, source_target_pairs={{0,128},{64,192},{128,0},{192,64},{1,129},{65,193},{129,1},{193,65... | collective-permute-start | bytes 1179656 | tf_op jit(solution)/shard_map/ppermute | solution.py:346
  157.7 32.3 %all-to-all-start.4 = ((bf16[64,8,768]{2,1,0:T(8,128)(2,1)}), bf16[64,8,768]{2,1,0:T(8,128)(2,1)S(1)}, u32[]{:S(2)}, u32[]{:S(2)}) async-start(bf16[64,8,768]{2,1,0:T(8,128)(2,1)} %join_in.1), calls=%async_computation.4 | async-start | bytes 1572864 | tf_op jit(solution)/shard_map/all_to_all | solution.py:353
  175.4 8.4 %copy-start.1 = (bf16[256,768]{1,0:T(8,128)(2,1)S(1)}, bf16[256,768]{1,0:T(8,128)(2,1)}, u32[]{:S(2)}) copy-start(bf16[256,768]{1,0:T(8,128)(2,1)} %refs_1_.3) | copy-start | bytes 1179652
  192.8 2.4 %collective-permute-start.13 = (bf16[256,768]{1,0:T(8,128)(2,1)S(1)}, bf16[256,768]{1,0:T(8,128)(2,1)S(1)}, u32[]{:S(2)}, u32[]{:S(2)}) collective-permute-start(bf16[256,768]{1,0:T(8,128)(2,1)S(1)} %get-tuple-element.77), channel_id=1, source_target_pairs={{0,1},{1,0},{2,3},{3,2},{4,5},{5,4},{6,7},{7,6},{8,9},{9,8},{10,11... | collective-permute-start | bytes 1179656 | tf_op jit(solution)/shard_map/ppermute | solution.py:342
  196.0 22.5 %all-to-all-start.5 = ((bf16[64,4,768]{2,1,0:T(4,128)(2,1)}), bf16[64,4,768]{2,1,0:T(4,128)(2,1)S(1)}, u32[]{:S(2)}, u32[]{:S(2)}) async-start(bf16[64,4,768]{2,1,0:T(4,128)(2,1)} %fold.1), calls=%async_computation.5 | async-start | bytes 786432 | tf_op jit(solution)/shard_map/all_to_all | solution.py:353
  218.7 5.3 %collective-permute-start.14 = (f32[4,768]{1,0:T(4,128)S(1)}, f32[4,768]{1,0:T(4,128)S(1)}, u32[]{:S(2)}, u32[]{:S(2)}) collective-permute-start(f32[4,768]{1,0:T(4,128)S(1)} %convert_reduce_fusion), channel_id=1, source_target_pairs={{0,128},{128,0},{1,129},{129,1},{2,130},{130,2},{3,131},{131,3},{4... | collective-permute-start | bytes 36872 | tf_op jit(solution)/shard_map/ppermute | solution.py:342
  (3 other events, 8.1 us)
